TPU v7x, 32 devices: a whole 2x2x4 slice. The times are simulated.
32 devices in a mesh: group: 4 (over y, x), inner: 8 (over z, core).
Axes of the slice: x: 2, y: 2, z: 4, core: 2. Of those that a mesh axis runs over, the one named last changes fastest.
Arguments:
- node_feats: bfloat16 [196608, 256], P(('group', 'inner')), may hold values from -6 to 6
- adj_tiles: bfloat16 [196608, 512], P(('group', 'inner')), may hold values from -0.25 to 0.25
- live_clusters: int32 [32], P(('group', 'inner')), may hold values from 4 to 12, as said below
- req_rows: int32 [32, 32, 16], P(('group', 'inner')), may hold values from 0 to 6143
- req_count: int32 [32, 32], P(('group', 'inner')), may hold values from 0 to 16, as said below
- req_target: int32 [32, 32, 16], P(('group', 'inner')), may hold values from 0 to 6143
- req_weight: float32 [32, 32, 16], P(('group', 'inner')), may hold values from 0.05 to 1
- hist_emb: bfloat16 [196608, 256], P(('group', 'inner')), may hold values from -6 to 6
- hist_grad: bfloat16 [196608, 256], P(('group', 'inner')), may hold values from -6 to 6
- layer_weight: bfloat16 [256, 256], replicated, may hold values from -0.375 to 0.375
- layer_bias: float32 [256], replicated, may hold values from -4 to 4
- cotangent: bfloat16 [196608, 256], P(('group', 'inner')), may hold values from -6 to 6
Outputs:
- input_grad: bfloat16 [196608, 256], P(('group', 'inner'))
- weight_grad: float32 [256, 256], replicated
- bias_grad: float32 [256], replicated
- owner_grad: bfloat16 [196608, 256], P(('group', 'inner'))
Inputs may be any that keep to these rules, and one draw needn't show every extreme that they name: `live_clusters`: some device has all 12 cluster slots filled and some has only the fewest. `req_count`: in every draw each requesting device fills all 16 slots to some owner, and some owner receives 16 used slots from every device.
All inputs are finite; a program needn't handle non-finite values.
Results may differ from a plain program's by a relative error of at most 0.0063.
Values may be sent and summed in bfloat16 or wider, within the bound.
A program may use at most 128 MiB of HBM per device.

v0:
```python
import math
import jax
import jax.numpy as jnp
from jax import lax
from jax.sharding import PartitionSpec as P


def gelu_slope(values):
    root_coef = math.sqrt(2.0 / math.pi)
    cube_coef = 0.044715
    tangent = jnp.tanh(root_coef * (values + cube_coef * values * values * values))
    return 0.5 * (1.0 + tangent) + 0.5 * values * (1.0 - tangent * tangent) * root_coef * (
        1.0 + 3.0 * cube_coef * values * values
    )


def on_device(
    node_feats,
    adj_tiles,
    live_clusters,
    req_rows,
    req_count,
    req_target,
    req_weight,
    hist_emb,
    hist_grad,
    layer_weight,
    layer_bias,
    cotangent,
):
    nodes_dev, width = node_feats.shape
    cluster = adj_tiles.shape[1]
    clusters = nodes_dev // cluster
    asked = req_rows[0]
    peers, slots = asked.shape
    groups = lax.axis_size("group")
    members = lax.axis_size("inner")
    slot_used = jnp.arange(slots)[None, :] < req_count[0][:, None]
    slot_scale = jnp.where(slot_used, req_weight[0], jnp.float32(0.0))
    target_ids = req_target[0]
    targets = target_ids.reshape(-1)
    wanted = lax.all_to_all(asked, ("group", "inner"), split_axis=0, concat_axis=0, tiled=True)
    emb_rows = hist_emb[wanted]
    grad_rows = hist_grad[wanted]
    got_emb = lax.all_to_all(emb_rows, ("group", "inner"), split_axis=0, concat_axis=0, tiled=True)
    got_grad = lax.all_to_all(
        grad_rows, ("group", "inner"), split_axis=0, concat_axis=0, tiled=True
    )
    weights_col = slot_scale.reshape(-1, 1)
    adj_blocks = adj_tiles.reshape(clusters, cluster, cluster)
    local_sum = jnp.einsum(
        "cij,cjf->cif",
        adj_blocks,
        node_feats.reshape(clusters, cluster, width),
        preferred_element_type=jnp.float32,
    ).reshape(nodes_dev, width)
    comp_emb = jax.ops.segment_sum(
        weights_col * got_emb.reshape(-1, width).astype(jnp.float32),
        targets,
        num_segments=nodes_dev,
    )
    aggregate = (local_sum + comp_emb).astype(jnp.bfloat16)
    pre_act = jnp.dot(aggregate, layer_weight, preferred_element_type=jnp.float32) + layer_bias
    live_rows = (jnp.arange(nodes_dev) // cluster < live_clusters[0]).astype(jnp.float32)[:, None]
    grad_pre = cotangent.astype(jnp.float32) * gelu_slope(pre_act) * live_rows
    grad_low = grad_pre.astype(jnp.bfloat16)
    weight_part = jnp.einsum("nf,ng->fg", aggregate, grad_low, preferred_element_type=jnp.float32)
    bias_part = jnp.sum(grad_pre, axis=0)
    feat_grad = jnp.dot(grad_low, layer_weight.T, preferred_element_type=jnp.float32).astype(
        jnp.bfloat16
    )
    message = (slot_scale[:, :, None] * feat_grad[target_ids].astype(jnp.float32)).astype(
        jnp.bfloat16
    )
    arrived = lax.all_to_all(message, ("group", "inner"), split_axis=0, concat_axis=0, tiled=True)
    owner_grad = jax.ops.segment_sum(
        arrived.reshape(-1, width).astype(jnp.float32), wanted.reshape(-1), num_segments=nodes_dev
    ).astype(jnp.bfloat16)
    comp_grad = jax.ops.segment_sum(
        weights_col * got_grad.reshape(-1, width).astype(jnp.float32),
        targets,
        num_segments=nodes_dev,
    ).astype(jnp.bfloat16)
    back_sum = jnp.einsum(
        "cji,cjf->cif",
        adj_blocks,
        feat_grad.reshape(clusters, cluster, width),
        preferred_element_type=jnp.float32,
    ).reshape(nodes_dev, width)
    back_sum = back_sum + jnp.dot(comp_grad, layer_weight.T, preferred_element_type=jnp.float32)
    input_grad = (back_sum * live_rows).astype(jnp.bfloat16)
    weight_sum, bias_sum = lax.psum((weight_part, bias_part), ("group", "inner"))
    norm_factor = float(nodes_dev * groups * members) ** (-0.5)
    return (input_grad, weight_sum * norm_factor, bias_sum * norm_factor, owner_grad)


def solution(mesh):
    return jax.shard_map(
        on_device,
        mesh=mesh,
        in_specs=(
            P(("group", "inner"), None),
            P(("group", "inner"), None),
            P(("group", "inner")),
            P(("group", "inner"), None, None),
            P(("group", "inner"), None),
            P(("group", "inner"), None, None),
            P(("group", "inner"), None, None),
            P(("group", "inner"), None),
            P(("group", "inner"), None),
            P(),
            P(),
            P(("group", "inner"), None),
        ),
        out_specs=(P(("group", "inner"), None), P(), P(), P(("group", "inner"), None)),
        check_vma=False,
    )
```

profile of v0, /device:TPU:0, one launch (start us, length us, event | category | flops | bytes accessed | tf_op | source)
XLA Modules:
  0.0 225.8 jit_solution(15960307121424035594)
XLA Ops:
  7.2 1.5 copy.31
  8.7 7.3 %all-to-all-start = ((s32[32,1,16]{2,1,0:T(1,128)}), s32[32,1,16]{2,1,0:T(1,128)S(1)}, u32[]{:S(2)}, u32[]{:S(2)}) async-start(s32[32,1,16]{2,1,0:T(1,128)} %bitcast.4), calls=%async_computation | async-start | bytes 32768 | tf_op jit(solution)/shard_map/all_to_all | solution.py:42
  16.7 0.7 bitcast_select_fusion
  17.4 0.8 copy.30
  19.0 0.8 copy.28
  20.6 0.7 copy.34
  21.3 1.8 all-to-all-done
  23.2 4.5 %gather_fusion = bf16[512,256]{1,0:T(8,128)(2,1)} fusion(bf16[6144,256]{1,0:T(8,128)(2,1)} %param.19, s32[1024]{0:T(1024)S(1)} %pad_clamp_fusion.1), kind=kCustom, calls=%fused_computation | custom fusion | bytes 526336 | tf_op jit(solution)/shard_map/gather | solution.py:43
  27.7 4.1 %all-to-all-start.1 = ((bf16[32,16,256]{2,1,0:T(8,128)(2,1)}), bf16[32,16,256]{2,1,0:T(8,128)(2,1)S(1)}, u32[]{:S(2)}, u32[]{:S(2)}) async-start(bf16[32,16,256]{2,1,0:T(8,128)(2,1)} %bitcast.48), calls=%async_computation.1 | async-start | bytes 524288 | tf_op jit(solution)/shard_map/all_to_all | solution.py:45
  31.8 7.2 %fusion.30 = f32[12,512,256]{2,1,0:T(8,128)} fusion(bf16[12,512,512]{2,1,0:T(8,128)(2,1)} %bitcast.40, bf16[12,512,256]{2,1,0:T(8,128)(2,1)S(1)} %bitcast.39), kind=kOutput, calls=%fused_computation.58 | convolution fusion | flops 1610612736 | bytes 15728640 | tf_op jit(solution)/shard_map/cij,cjf->cif/dot_general | solution.py:51
  39.5 2.0 reduce.3
  41.5 1.4 reshape.207
  42.9 4.5 %gather_fusion.1 = bf16[512,256]{1,0:T(8,128)(2,1)} fusion(bf16[6144,256]{1,0:T(8,128)(2,1)} %param.20, s32[1024]{0:T(1024)S(1)} %pad_clamp_fusion.1), kind=kCustom, calls=%fused_computation.1 | custom fusion | bytes 526336 | tf_op jit(solution)/shard_map/gather | solution.py:44
  47.4 0.7 copy-done.3
  48.1 5.8 %all-to-all-start.2 = ((bf16[32,16,256]{2,1,0:T(8,128)(2,1)}), bf16[32,16,256]{2,1,0:T(8,128)(2,1)S(1)}, u32[]{:S(2)}, u32[]{:S(2)}) async-start(bf16[32,16,256]{2,1,0:T(8,128)(2,1)} %bitcast.46), calls=%async_computation.2 | async-start | bytes 524288 | tf_op jit(solution)/shard_map/all_to_all | solution.py:46
  54.0 9.0 %scatter_custom_fusion = f32[6144,256]{1,0:T(8,128)} fusion(f32[6144,256]{1,0:T(8,128)} %bitcast.42, s32[512]{0:T(512)S(1)} %reshape.191, bf16[512,256]{1,0:T(8,128)(2,1)} %bitcast.47, f32[512]{0:T(512)S(1)} %broadcast_select_fusion), kind=kCustom, calls=%fused_computation.36 | custom fusion | flops 393216 | bytes 6555648 | tf_op jit(solution)/shard_map/scatter-add | solution.py:57
  63.0 8.5 %fusion.29 = (f32[256]{0:T(256)}, bf16[6144,256]{1,0:T(8,128)(2,1)S(1)}) fusion(f32[6144]{0:T(1024)} %fusion.28, f32[256]{0:T(256)} %param.22, bf16[256,256]{1,0:T(8,128)(2,1)S(1)} %copy-done.4, f32[6144,256]{1,0:T(8,128)} %scatter_custom_fusion, bf16[6144,256]{1,0:T(8,128)(2,1)} %param.23), kind=kOutput, calls=%fused_computation.57 | convolution fusion | flops 843054848 | bytes 12740608 | tf_op jit(solution)/shard_map/dot_general | solution.py:63
  71.4 1.7 copy-done.2
  73.1 1.7 fusion.14
  74.8 4.6 %convolution_convert_fusion = bf16[6144,256]{1,0:T(8,128)(2,1)} fusion(bf16[256,256]{1,0:T(8,128)(2,1)S(1)} %copy-done.4, bf16[6144,256]{1,0:T(8,128)(2,1)} %copy-done.2), kind=kOutput, calls=%fused_computation.12 | convolution fusion | flops 806879232 | bytes 6422528 | tf_op jit(solution)/shard_map/dot_general | solution.py:69
  79.4 8.2 %convolution_bitcast_fusion = f32[12,512,256]{1,2,0:T(8,128)} fusion(bf16[12,512,256]{2,1,0:T(8,128)(2,1)} %bitcast.43, bf16[12,512,512]{2,1,0:T(8,128)(2,1)} %bitcast.41), kind=kOutput, calls=%fused_computation.25 | convolution fusion | flops 1610612736 | bytes 15728640 | tf_op jit(solution)/shard_map/cji,cjf->cif/dot_general | solution.py:84
  87.7 4.5 %gather_fusion.2 = bf16[512,256]{1,0:T(8,128)(2,1)} fusion(bf16[6144,256]{1,0:T(8,128)(2,1)} %convolution_convert_fusion, s32[1024]{0:T(1024)S(1)} %pad_clamp_fusion), kind=kCustom, calls=%fused_computation.2 | custom fusion | bytes 526336 | tf_op jit(solution)/shard_map/gather | solution.py:72
  92.2 6.6 %copy.33 = f32[12,512,256]{2,1,0:T(8,128)} copy(f32[12,512,256]{1,2,0:T(8,128)} %convolution_bitcast_fusion) | data formatting | bytes 12582912 | tf_op jit(solution)/shard_map/cji,cjf->cif/dot_general | solution.py:84
  98.8 1.8 fusion.20
  100.5 6.0 %all-to-all-start.3 = ((bf16[32,16,256]{2,1,0:T(8,128)(2,1)}), bf16[32,16,256]{2,1,0:T(8,128)(2,1)}, u32[]{:S(2)}, u32[]{:S(2)}) async-start(bf16[32,16,256]{2,1,0:T(8,128)(2,1)} %fusion.20), calls=%async_computation.3 | async-start | bytes 524288 | tf_op jit(solution)/shard_map/all_to_all | solution.py:75
  106.5 6.6 %scatter_custom_fusion.1 = f32[6144,256]{1,0:T(8,128)} fusion(s32[512]{0:T(512)} %copy-done.8, f32[]{:T(128)} %constant.13.clone.1, bf16[512,256]{1,0:T(8,128)(2,1)S(1)} %bitcast.45, f32[512]{0:T(512)} %copy-done.7), kind=kCustom, calls=%fused_computation.23 | custom fusion | flops 393216 | bytes 6556160 | tf_op jit(solution)/shard_map/scatter-add | solution.py:79
  113.1 7.6 %fusion.1 = bf16[6144,256]{1,0:T(8,128)(2,1)} fusion(f32[6144,256]{1,0:T(8,128)} %bitcast.44, bf16[256,256]{1,0:T(8,128)(2,1)S(1)} %copy-done.4, f32[6144,256]{1,0:T(8,128)} %scatter_custom_fusion.1, f32[6144]{0:T(1024)} %fusion.28), kind=kOutput, calls=%fused_computation.11 | convolution fusion | flops 811597824 | bytes 15884288 | tf_op jit(solution)/shard_map/dot_general | solution.py:90
  120.7 40.5 %psum.15 = f32[256]{0:T(256)S(1)} all-reduce(f32[256]{0:T(256)S(1)} %copy-done.9), channel_id=1, replica_groups=mesh['group'=4,'inner'=8] {'group','inner'}, use_global_device_ids=true, to_apply=%region_4.5 | all-reduce | flops 256 | bytes 2048 | tf_op jit(solution)/shard_map/psum | solution.py:92
  161.7 44.1 %all-reduce.2.cloned.1.call-done = f32[256,256]{1,0:T(8,128)} async-done(((f32[256,256]{1,0:T(8,128)}), f32[256,256]{1,0:T(8,128)}) %all-reduce.2.cloned.1.call-update) | async-done | bytes 262160 | tf_op jit(solution)/shard_map/psum | solution.py:92
  205.8 1.7 broadcast_multiply_fusion
  207.5 6.7 %scatter_custom_fusion.2 = f32[6144,256]{1,0:T(8,128)} fusion(s32[512]{0:T(512)} %reshape.207, f32[]{:T(128)} %constant.13.clone.1, bf16[512,256]{1,0:T(8,128)(2,1)} %bitcast.21), kind=kCustom, calls=%fused_computation.21 | custom fusion | flops 262144 | bytes 6554112 | tf_op jit(solution)/shard_map/scatter-add | solution.py:76
  214.2 4.8 %convert_element_type.67 = bf16[6144,256]{1,0:T(8,128)(2,1)} convert(f32[6144,256]{1,0:T(8,128)} %scatter_custom_fusion.2) | non-fusion elementwise | flops 1572864 | bytes 9437184 | tf_op jit(solution)/shard_map/convert_element_type | solution.py:78
  (38 shorter events, 3.0 us)
Async XLA Ops:
  7.2 24.6 %copy-start = (bf16[6144,256]{1,0:T(8,128)(2,1)S(1)}, bf16[6144,256]{1,0:T(8,128)(2,1)}, u32[]{:S(2)}) copy-start(bf16[6144,256]{1,0:T(8,128)(2,1)} %param.12) | copy-start | bytes 9437188
  8.7 14.4 %all-to-all-start = ((s32[32,1,16]{2,1,0:T(1,128)}), s32[32,1,16]{2,1,0:T(1,128)S(1)}, u32[]{:S(2)}, u32[]{:S(2)}) async-start(s32[32,1,16]{2,1,0:T(1,128)} %bitcast.4), calls=%async_computation | async-start | bytes 32768 | tf_op jit(solution)/shard_map/all_to_all | solution.py:42
  20.5 33.5 %copy-start.7 = (f32[512]{0:T(512)}, f32[512]{0:T(512)S(1)}, u32[]{:S(2)}) copy-start(f32[512]{0:T(512)S(1)} %broadcast_select_fusion) | copy-start | bytes 6148
  20.6 33.4 %copy-start.8 = (s32[512]{0:T(512)}, s32[512]{0:T(512)S(1)}, u32[]{:S(2)}) copy-start(s32[512]{0:T(512)S(1)} %reshape.191) | copy-start | bytes 6148
  23.1 4.6 %copy-start.5 = (s32[32,1,16]{2,1,0:T(1,128)}, s32[32,1,16]{2,1,0:T(1,128)S(1)}, u32[]{:S(2)}) copy-start(s32[32,1,16]{2,1,0:T(1,128)S(1)} %all-to-all-done) | copy-start | bytes 6148
  27.7 19.7 %all-to-all-start.1 = ((bf16[32,16,256]{2,1,0:T(8,128)(2,1)}), bf16[32,16,256]{2,1,0:T(8,128)(2,1)S(1)}, u32[]{:S(2)}, u32[]{:S(2)}) async-start(bf16[32,16,256]{2,1,0:T(8,128)(2,1)} %bitcast.48), calls=%async_computation.1 | async-start | bytes 524288 | tf_op jit(solution)/shard_map/all_to_all | solution.py:45
  39.0 24.0 %copy-start.4 = (bf16[256,256]{1,0:T(8,128)(2,1)S(1)}, bf16[256,256]{1,0:T(8,128)(2,1)}, u32[]{:S(2)}) copy-start(bf16[256,256]{1,0:T(8,128)(2,1)} %param.21) | copy-start | bytes 393220
  47.4 0.7 copy-start.3
  48.1 52.4 %all-to-all-start.2 = ((bf16[32,16,256]{2,1,0:T(8,128)(2,1)}), bf16[32,16,256]{2,1,0:T(8,128)(2,1)S(1)}, u32[]{:S(2)}, u32[]{:S(2)}) async-start(bf16[32,16,256]{2,1,0:T(8,128)(2,1)} %bitcast.46), calls=%async_computation.2 | async-start | bytes 524288 | tf_op jit(solution)/shard_map/all_to_all | solution.py:46
  54.0 151.8 %all-reduce.2.cloned.1.call-start = ((), (), s32[]{:S(2)}) async-start(), calls=%async_computation.4 | async-start | bytes 524288 | tf_op jit(solution)/shard_map/psum | solution.py:92
  63.0 10.1 %copy-start.1 = (f32[6144,256]{1,0:T(8,128)S(1)}, f32[6144,256]{1,0:T(8,128)}, u32[]{:S(2)}) copy-start(f32[6144,256]{1,0:T(8,128)} %scatter_custom_fusion) | copy-start | bytes 18874372
  71.4 1.7 copy-start.2
  92.1 6.6 %copy-start.6 = (f32[32,16]{1,0:T(8,128)S(1)}, f32[32,16]{1,0:T(8,128)}, u32[]{:S(2)}) copy-start(f32[32,16]{1,0:T(8,128)} %copy.34) | copy-start | bytes 6148
  100.5 106.9 %all-to-all-start.3 = ((bf16[32,16,256]{2,1,0:T(8,128)(2,1)}), bf16[32,16,256]{2,1,0:T(8,128)(2,1)}, u32[]{:S(2)}, u32[]{:S(2)}) async-start(bf16[32,16,256]{2,1,0:T(8,128)(2,1)} %fusion.20), calls=%async_computation.3 | async-start | bytes 524288 | tf_op jit(solution)/shard_map/all_to_all | solution.py:75
  113.1 7.6 %copy-start.9 = (f32[256]{0:T(256)S(1)}, f32[256]{0:T(256)}, u32[]{:S(2)}) copy-start(f32[256]{0:T(256)} %get-tuple-element.4) | copy-start | bytes 3076
Sparse Core Ops, SparseCore 0:
  79.5 126.2 all-reduce.1
where the time goes:
time: 227 us; the launch traced here: 226 us
  waiting for transfers between devices  45.8 us (20%)
  blocking collectives  40.5 us (18%)
  matrix products  37.8 us (17%)
  other arithmetic  35.1 us (15%)
  local copies, waits for them, and re-layouts  28.6 us (13%)
  starting transfers between devices  23.2 us (10%)
  between operations  14.8 us (7%)
    psum x1, waiting for transfers between devices, on_device(): lax.psum((weight_part, bias_part), ('group', 'inner'))  44.1 us
    psum x1, blocking collectives, on_device(): lax.psum((weight_part, bias_part), ('group', 'inner'))  40.5 us
    scatter-add x1, other arithmetic, on_device(): jax.ops.segment_sum(weights_col * got_emb.reshape(-1, width).astype(jnp.f...  8.96 us
    dot_general x1, matrix products, on_device(): jnp.dot(aggregate, layer_weight, preferred_element_type=jnp.float32)  8.45 us
    dot_general x1, matrix products, on_device(): jnp.einsum('cji,cjf->cif', adj_blocks, feat_grad.reshape(clusters, cluste...  8.25 us
    dot_general x1, matrix products, on_device(): jnp.dot(comp_grad, layer_weight.T, preferred_element_type=jnp.float32)  7.58 us
    all_to_all x1, starting transfers between devices, on_device(): lax.all_to_all(asked, ('group', 'inner'), split_axis=0, concat_axis=0, ti...  7.3 us
    dot_general x1, matrix products, on_device(): jnp.einsum('cij,cjf->cif', adj_blocks, node_feats.reshape(clusters, clust...  7.24 us
  transfers between devices with their start and end apart: 5, of which 2 were waited for; matrix products, arithmetic and copies ran while one was open for 36% of the time, Pallas kernels for 0%

commit v1 on v0

--- a/solution.py
+++ b/solution.py
@@ -89,7 +89,7 @@
     ).reshape(nodes_dev, width)
     back_sum = back_sum + jnp.dot(comp_grad, layer_weight.T, preferred_element_type=jnp.float32)
     input_grad = (back_sum * live_rows).astype(jnp.bfloat16)
-    weight_sum, bias_sum = lax.psum((weight_part, bias_part), ("group", "inner"))
+    weight_sum, bias_sum = lax.psum(lax.psum((weight_part, bias_part), "inner"), "group")
     norm_factor = float(nodes_dev * groups * members) ** (-0.5)
     return (input_grad, weight_sum * norm_factor, bias_sum * norm_factor, owner_grad)
 

time: 227 us -> 202 us (0.89)
  blocking collectives: 40.5 us -> 23.5 us
  waiting for transfers between devices: 45.8 us -> 37.8 us
    psum x1 -> x2, blocking collectives: 40.5 us -> 23.5 us  [the longest x1 13.7 us: on_device(): lax.psum((weight_part, bias_part), 'inner')]
    psum x1 -> x2, waiting for transfers between devices: 44.1 us -> 36 us  [the longest x1 22.6 us: on_device(): lax.psum((weight_part, bias_part), 'inner')]
  transfers between devices with their start and end apart: 5 -> 6, of which waited for: 2 -> 3; matrix products, arithmetic and copies ran while one was open for 36% -> 41% of each run, Pallas kernels for 0% -> 0%
where the time goes in v1:
time: 202 us; the launch traced here: 201 us
  waiting for transfers between devices  37.8 us (19%)
  matrix products  37.8 us (19%)
  other arithmetic  35.1 us (17%)
  local copies, waits for them, and re-layouts  28.6 us (14%)
  blocking collectives  23.5 us (12%)
  starting transfers between devices  23.3 us (12%)
  between operations  14.8 us (7%)
    psum x1, waiting for transfers between devices, on_device(): lax.psum((weight_part, bias_part), 'inner')  22.6 us
    psum x1, blocking collectives, on_device(): lax.psum((weight_part, bias_part), 'inner')  13.7 us
    psum x1, waiting for transfers between devices, on_device(): lax.psum(lax.psum((weight_part, bias_part), 'inner'), 'group')  13.5 us
    psum x1, blocking collectives, on_device(): lax.psum(lax.psum((weight_part, bias_part), 'inner'), 'group')  9.82 us
    scatter-add x1, other arithmetic, on_device(): jax.ops.segment_sum(weights_col * got_emb.reshape(-1, width).astype(jnp.f...  8.97 us
    dot_general x1, matrix products, on_device(): jnp.dot(aggregate, layer_weight, preferred_element_type=jnp.float32)  8.45 us
    dot_general x1, matrix products, on_device(): jnp.einsum('cji,cjf->cif', adj_blocks, feat_grad.reshape(clusters, cluste...  8.24 us
    dot_general x1, matrix products, on_device(): jnp.dot(comp_grad, layer_weight.T, preferred_element_type=jnp.float32)  7.56 us
  transfers between devices with their start and end apart: 6, of which 3 were waited for; matrix products, arithmetic and copies ran while one was open for 41% of the time, Pallas kernels for 0%

profile of v1, /device:TPU:0, one launch (start us, length us, event | category | flops | bytes accessed | tf_op | source)
XLA Modules:
  0.0 200.9 jit_solution(7016713375051704175)
XLA Ops:
  7.2 1.5 copy.31
  8.7 7.3 %all-to-all-start = ((s32[32,1,16]{2,1,0:T(1,128)}), s32[32,1,16]{2,1,0:T(1,128)S(1)}, u32[]{:S(2)}, u32[]{:S(2)}) async-start(s32[32,1,16]{2,1,0:T(1,128)} %bitcast.4), calls=%async_computation | async-start | bytes 32768 | tf_op jit(solution)/shard_map/all_to_all | solution.py:42
  16.7 0.7 bitcast_select_fusion
  17.4 0.8 copy.30
  19.0 0.8 copy.28
  21.3 1.8 all-to-all-done
  23.2 4.5 %gather_fusion = bf16[512,256]{1,0:T(8,128)(2,1)} fusion(bf16[6144,256]{1,0:T(8,128)(2,1)} %param.19, s32[1024]{0:T(1024)S(1)} %pad_clamp_fusion.1), kind=kCustom, calls=%fused_computation | custom fusion | bytes 526336 | tf_op jit(solution)/shard_map/gather | solution.py:43
  27.7 4.1 %all-to-all-start.1 = ((bf16[32,16,256]{2,1,0:T(8,128)(2,1)}), bf16[32,16,256]{2,1,0:T(8,128)(2,1)S(1)}, u32[]{:S(2)}, u32[]{:S(2)}) async-start(bf16[32,16,256]{2,1,0:T(8,128)(2,1)} %bitcast.48), calls=%async_computation.1 | async-start | bytes 524288 | tf_op jit(solution)/shard_map/all_to_all | solution.py:45
  31.8 7.2 %fusion.30 = f32[12,512,256]{2,1,0:T(8,128)} fusion(bf16[12,512,512]{2,1,0:T(8,128)(2,1)} %bitcast.40, bf16[12,512,256]{2,1,0:T(8,128)(2,1)S(1)} %bitcast.39), kind=kOutput, calls=%fused_computation.58 | convolution fusion | flops 1610612736 | bytes 15728640 | tf_op jit(solution)/shard_map/cij,cjf->cif/dot_general | solution.py:51
  39.5 2.0 %reduce.3 = s32[32,16]{1,0:T(8,128)} reduce(s32[32,1,16]{2,1,0:T(1,128)} %copy-done.5, s32[]{:T(128)} %broadcast.135), dimensions={1}, to_apply=%all_to_all.18.reduce_sub_computation.3 | reduce | bytes 4100 | tf_op jit(solution)/shard_map/all_to_all | solution.py:42
  41.5 1.4 reshape.207
  42.9 4.5 %gather_fusion.1 = bf16[512,256]{1,0:T(8,128)(2,1)} fusion(bf16[6144,256]{1,0:T(8,128)(2,1)} %param.20, s32[1024]{0:T(1024)S(1)} %pad_clamp_fusion.1), kind=kCustom, calls=%fused_computation.1 | custom fusion | bytes 526336 | tf_op jit(solution)/shard_map/gather | solution.py:44
  48.1 5.8 %all-to-all-start.2 = ((bf16[32,16,256]{2,1,0:T(8,128)(2,1)}), bf16[32,16,256]{2,1,0:T(8,128)(2,1)S(1)}, u32[]{:S(2)}, u32[]{:S(2)}) async-start(bf16[32,16,256]{2,1,0:T(8,128)(2,1)} %bitcast.46), calls=%async_computation.2 | async-start | bytes 524288 | tf_op jit(solution)/shard_map/all_to_all | solution.py:46
  54.0 9.0 %scatter_custom_fusion = f32[6144,256]{1,0:T(8,128)} fusion(f32[6144,256]{1,0:T(8,128)} %bitcast.42, s32[512]{0:T(512)S(1)} %reshape.191, bf16[512,256]{1,0:T(8,128)(2,1)} %bitcast.47, f32[512]{0:T(512)S(1)} %broadcast_select_fusion), kind=kCustom, calls=%fused_computation.36 | custom fusion | flops 393216 | bytes 6555648 | tf_op jit(solution)/shard_map/scatter-add | solution.py:57
  63.0 8.5 %fusion.29 = (f32[256]{0:T(256)}, bf16[6144,256]{1,0:T(8,128)(2,1)S(1)}) fusion(f32[6144]{0:T(1024)} %fusion.28, f32[256]{0:T(256)} %param.22, bf16[256,256]{1,0:T(8,128)(2,1)S(1)} %copy-done.4, f32[6144,256]{1,0:T(8,128)} %scatter_custom_fusion, bf16[6144,256]{1,0:T(8,128)(2,1)} %param.23), kind=kOutput, calls=%fused_computation.57 | convolution fusion | flops 843054848 | bytes 12740608 | tf_op jit(solution)/shard_map/dot_general | solution.py:63
  71.4 1.7 copy-done.2
  73.1 1.7 fusion.14
  74.8 4.6 %convolution_convert_fusion = bf16[6144,256]{1,0:T(8,128)(2,1)} fusion(bf16[256,256]{1,0:T(8,128)(2,1)S(1)} %copy-done.4, bf16[6144,256]{1,0:T(8,128)(2,1)} %copy-done.2), kind=kOutput, calls=%fused_computation.12 | convolution fusion | flops 806879232 | bytes 6422528 | tf_op jit(solution)/shard_map/dot_general | solution.py:69
  79.4 8.2 %convolution_bitcast_fusion = f32[12,512,256]{1,2,0:T(8,128)} fusion(bf16[12,512,256]{2,1,0:T(8,128)(2,1)} %bitcast.43, bf16[12,512,512]{2,1,0:T(8,128)(2,1)} %bitcast.41), kind=kOutput, calls=%fused_computation.25 | convolution fusion | flops 1610612736 | bytes 15728640 | tf_op jit(solution)/shard_map/cji,cjf->cif/dot_general | solution.py:84
  87.7 4.5 %gather_fusion.2 = bf16[512,256]{1,0:T(8,128)(2,1)} fusion(bf16[6144,256]{1,0:T(8,128)(2,1)} %convolution_convert_fusion, s32[1024]{0:T(1024)S(1)} %pad_clamp_fusion), kind=kCustom, calls=%fused_computation.2 | custom fusion | bytes 526336 | tf_op jit(solution)/shard_map/gather | solution.py:72
  92.1 6.6 %copy.33 = f32[12,512,256]{2,1,0:T(8,128)} copy(f32[12,512,256]{1,2,0:T(8,128)} %convolution_bitcast_fusion) | data formatting | bytes 12582912 | tf_op jit(solution)/shard_map/cji,cjf->cif/dot_general | solution.py:84
  98.8 1.8 fusion.20
  100.6 6.0 %all-to-all-start.3 = ((bf16[32,16,256]{2,1,0:T(8,128)(2,1)}), bf16[32,16,256]{2,1,0:T(8,128)(2,1)}, u32[]{:S(2)}, u32[]{:S(2)}) async-start(bf16[32,16,256]{2,1,0:T(8,128)(2,1)} %fusion.20), calls=%async_computation.3 | async-start | bytes 524288 | tf_op jit(solution)/shard_map/all_to_all | solution.py:75
  106.6 6.6 %scatter_custom_fusion.1 = f32[6144,256]{1,0:T(8,128)} fusion(s32[512]{0:T(512)} %copy-done.8, f32[]{:T(128)} %constant.13.clone.1, bf16[512,256]{1,0:T(8,128)(2,1)S(1)} %bitcast.45, f32[512]{0:T(512)} %copy-done.7), kind=kCustom, calls=%fused_computation.23 | custom fusion | flops 393216 | bytes 6556160 | tf_op jit(solution)/shard_map/scatter-add | solution.py:79
  113.2 22.6 %all-reduce.3.cloned.1.call-done = f32[256,256]{1,0:T(8,128)} async-done(((f32[256,256]{1,0:T(8,128)}), f32[256,256]{1,0:T(8,128)}) %all-reduce.3.cloned.1.call-update) | async-done | bytes 262160 | tf_op jit(solution)/shard_map/psum | solution.py:92
  135.8 7.6 %fusion.1 = bf16[6144,256]{1,0:T(8,128)(2,1)} fusion(f32[6144,256]{1,0:T(8,128)} %bitcast.44, bf16[256,256]{1,0:T(8,128)(2,1)S(1)} %copy-done.4, f32[6144,256]{1,0:T(8,128)} %scatter_custom_fusion.1, f32[6144]{0:T(1024)} %fusion.28), kind=kOutput, calls=%fused_computation.11 | convolution fusion | flops 811597824 | bytes 15884288 | tf_op jit(solution)/shard_map/dot_general | solution.py:90
  143.3 13.7 %psum.30 = f32[256]{0:T(256)S(1)} all-reduce(f32[256]{0:T(256)S(1)} %copy-done.9), channel_id=1, replica_groups=mesh['group'=4,'inner'=8] {'inner'}, use_global_device_ids=true, to_apply=%region_5.6 | all-reduce | flops 256 | bytes 2048 | tf_op jit(solution)/shard_map/psum | solution.py:92
  157.0 9.8 %psum.31 = f32[256]{0:T(256)S(1)} all-reduce(f32[256]{0:T(256)S(1)} %psum.30), channel_id=1, replica_groups=mesh['group'=4,'inner'=8] {'group'}, use_global_device_ids=true, to_apply=%region_6.7 | all-reduce | flops 256 | bytes 2048 | tf_op jit(solution)/shard_map/psum | solution.py:92
  167.4 13.5 %all-reduce.5.cloned.1.call-done = f32[256,256]{1,0:T(8,128)} async-done(((f32[256,256]{1,0:T(8,128)}), f32[256,256]{1,0:T(8,128)}) %all-reduce.5.cloned.1.call-update) | async-done | bytes 262160 | tf_op jit(solution)/shard_map/psum | solution.py:92
  180.8 1.7 broadcast_multiply_fusion
  182.5 6.8 %scatter_custom_fusion.2 = f32[6144,256]{1,0:T(8,128)} fusion(s32[512]{0:T(512)} %reshape.207, f32[]{:T(128)} %constant.13.clone.1, bf16[512,256]{1,0:T(8,128)(2,1)} %bitcast.21), kind=kCustom, calls=%fused_computation.21 | custom fusion | flops 262144 | bytes 6554112 | tf_op jit(solution)/shard_map/scatter-add | solution.py:76
  189.3 4.8 %convert_element_type.67 = bf16[6144,256]{1,0:T(8,128)(2,1)} convert(f32[6144,256]{1,0:T(8,128)} %scatter_custom_fusion.2) | non-fusion elementwise | flops 1572864 | bytes 9437184 | tf_op jit(solution)/shard_map/convert_element_type | solution.py:78
  (42 shorter events, 4.4 us)
Async XLA Ops:
  7.2 24.6 %copy-start = (bf16[6144,256]{1,0:T(8,128)(2,1)S(1)}, bf16[6144,256]{1,0:T(8,128)(2,1)}, u32[]{:S(2)}) copy-start(bf16[6144,256]{1,0:T(8,128)(2,1)} %param.12) | copy-start | bytes 9437188
  8.7 14.4 %all-to-all-start = ((s32[32,1,16]{2,1,0:T(1,128)}), s32[32,1,16]{2,1,0:T(1,128)S(1)}, u32[]{:S(2)}, u32[]{:S(2)}) async-start(s32[32,1,16]{2,1,0:T(1,128)} %bitcast.4), calls=%async_computation | async-start | bytes 32768 | tf_op jit(solution)/shard_map/all_to_all | solution.py:42
  20.5 33.4 %copy-start.7 = (f32[512]{0:T(512)}, f32[512]{0:T(512)S(1)}, u32[]{:S(2)}) copy-start(f32[512]{0:T(512)S(1)} %broadcast_select_fusion) | copy-start | bytes 6148
  20.6 33.4 %copy-start.8 = (s32[512]{0:T(512)}, s32[512]{0:T(512)S(1)}, u32[]{:S(2)}) copy-start(s32[512]{0:T(512)S(1)} %reshape.191) | copy-start | bytes 6148
  23.1 4.6 %copy-start.5 = (s32[32,1,16]{2,1,0:T(1,128)}, s32[32,1,16]{2,1,0:T(1,128)S(1)}, u32[]{:S(2)}) copy-start(s32[32,1,16]{2,1,0:T(1,128)S(1)} %all-to-all-done) | copy-start | bytes 6148
  27.7 19.7 %all-to-all-start.1 = ((bf16[32,16,256]{2,1,0:T(8,128)(2,1)}), bf16[32,16,256]{2,1,0:T(8,128)(2,1)S(1)}, u32[]{:S(2)}, u32[]{:S(2)}) async-start(bf16[32,16,256]{2,1,0:T(8,128)(2,1)} %bitcast.48), calls=%async_computation.1 | async-start | bytes 524288 | tf_op jit(solution)/shard_map/all_to_all | solution.py:45
  39.0 24.0 %copy-start.4 = (bf16[256,256]{1,0:T(8,128)(2,1)S(1)}, bf16[256,256]{1,0:T(8,128)(2,1)}, u32[]{:S(2)}) copy-start(bf16[256,256]{1,0:T(8,128)(2,1)} %param.21) | copy-start | bytes 393220
  47.4 0.7 copy-start.3
  48.1 52.5 %all-to-all-start.2 = ((bf16[32,16,256]{2,1,0:T(8,128)(2,1)}), bf16[32,16,256]{2,1,0:T(8,128)(2,1)S(1)}, u32[]{:S(2)}, u32[]{:S(2)}) async-start(bf16[32,16,256]{2,1,0:T(8,128)(2,1)} %bitcast.46), calls=%async_computation.2 | async-start | bytes 524288 | tf_op jit(solution)/shard_map/all_to_all | solution.py:46
  53.9 81.8 %all-reduce.3.cloned.1.call-start = ((), (), s32[]{:S(2)}) async-start(), calls=%async_computation.4 | async-start | bytes 524288 | tf_op jit(solution)/shard_map/psum | solution.py:92
  63.0 10.1 %copy-start.1 = (f32[6144,256]{1,0:T(8,128)S(1)}, f32[6144,256]{1,0:T(8,128)}, u32[]{:S(2)}) copy-start(f32[6144,256]{1,0:T(8,128)} %scatter_custom_fusion) | copy-start | bytes 18874372
  71.4 1.7 copy-start.2
  92.1 6.6 %copy-start.6 = (f32[32,16]{1,0:T(8,128)S(1)}, f32[32,16]{1,0:T(8,128)}, u32[]{:S(2)}) copy-start(f32[32,16]{1,0:T(8,128)} %copy.34) | copy-start | bytes 6148
  100.6 82.0 %all-to-all-start.3 = ((bf16[32,16,256]{2,1,0:T(8,128)(2,1)}), bf16[32,16,256]{2,1,0:T(8,128)(2,1)}, u32[]{:S(2)}, u32[]{:S(2)}) async-start(bf16[32,16,256]{2,1,0:T(8,128)(2,1)} %fusion.20), calls=%async_computation.3 | async-start | bytes 524288 | tf_op jit(solution)/shard_map/all_to_all | solution.py:75
  106.6 74.3 %all-reduce.5.cloned.1.call-start = ((), (), s32[]{:S(2)}) async-start(), calls=%async_computation.5 | async-start | bytes 524288 | tf_op jit(solution)/shard_map/psum | solution.py:92
  135.8 7.6 %copy-start.9 = (f32[256]{0:T(256)S(1)}, f32[256]{0:T(256)}, u32[]{:S(2)}) copy-start(f32[256]{0:T(256)} %get-tuple-element.4) | copy-start | bytes 3076
Sparse Core Ops, SparseCore 0:
  79.5 56.1 all-reduce.2
  138.9 41.8 all-reduce.4
